TPU v7x, 1024 devices: a whole 8x8x8 slice. The times are simulated.
1024 devices in a mesh: dp: 32 (over y_hi, x, core), seq: 32 (over z, y_lo).
Axes of the slice: x: 8, y: 8 (y_hi: 2, y_lo: 4; y = y_hi * 4 + y_lo), z: 8, core: 2. Of those that a mesh axis runs over, the one named last changes fastest.
Arguments:
- queries: bfloat16 [32, 512, 2048], P('dp', 'seq'), may hold values from -2 to 2
- enc_keys: bfloat16 [32, 4096, 2048], P('dp', 'seq'), may hold values from -1 to 1
- enc_values: bfloat16 [32, 4096, 2048], P('dp', 'seq'), may hold values from -0.375 to 0.375
- grad_context: bfloat16 [32, 512, 2048], P('dp', 'seq'), may hold values from -512 to 512
- enc_lengths: int32 [32], P('dp'), may hold values from 512 to 4096, as said below
Outputs:
- query_grad: bfloat16 [32, 512, 2048], P('dp', 'seq')
- key_grad: bfloat16 [32, 4096, 2048], P('dp', 'seq')
- value_grad: bfloat16 [32, 4096, 2048], P('dp', 'seq')
Inputs may be any that keep to these rules, and one draw needn't show every extreme that they name: `enc_lengths`: at least 512 live positions; some example has all 4096.
All inputs are finite; a program needn't handle non-finite values.
Results may differ from a plain program's by a relative error of at most 0.035.
Values may be sent and summed in bfloat16 or wider, within the bound.
A program may use at most 64 MiB of HBM per device.

v0:
```python
import jax
import jax.numpy as jnp
from jax import lax
from jax.sharding import PartitionSpec as P

HEADS = 8
HEAD_DIM = 256


masked_fill = -1e30


def joined(part, axis, combine):
    gathered = jax.tree.map(lambda a: lax.all_gather(a, axis), part)

    def take(source):
        return jax.tree.map(lambda a: lax.dynamic_index_in_dim(a, source, 0, False), gathered)

    return lax.fori_loop(
        1, lax.axis_size(axis), lambda source, state: combine(state, take(source)), take(0)
    )


def combine_pair(earlier, later):
    largest = jnp.maximum(earlier[0], later[0])
    totals = earlier[1] * jnp.exp(earlier[0] - largest) + later[1] * jnp.exp(later[0] - largest)
    return (largest, totals)


def body(queries, enc_keys, enc_values, grad_context, enc_lengths):
    gathered_queries, gathered_grads = (
        lax.all_gather(queries, "seq", axis=1, tiled=True),
        lax.all_gather(grad_context, "seq", axis=1, tiled=True),
    )
    dec_rows = gathered_queries.shape[1]
    enc_rows = enc_keys.shape[1]
    query_heads = gathered_queries.reshape(dec_rows, HEADS, HEAD_DIM)
    grad_heads = gathered_grads.reshape(dec_rows, HEADS, HEAD_DIM)
    key_heads = enc_keys.reshape(enc_rows, HEADS, HEAD_DIM)
    value_heads = enc_values.reshape(enc_rows, HEADS, HEAD_DIM)
    positions = lax.axis_index("seq") * enc_rows + jnp.arange(enc_rows, dtype=jnp.int32)
    live_keys = positions < enc_lengths[0]
    scores = jnp.einsum("qhd,khd->hqk", query_heads, key_heads, preferred_element_type=jnp.float32)
    masked = jnp.where(live_keys, scores, masked_fill)
    local_top = jnp.max(masked, -1)
    shifted = jnp.where(live_keys, jnp.exp(masked - local_top[..., None]), 0.0)
    local_total = jnp.sum(shifted, -1)
    weight_grad = jnp.einsum(
        "qhd,khd->hqk", grad_heads, value_heads, preferred_element_type=jnp.float32
    )
    largest, totals = joined((local_top, local_total), "seq", combine_pair)
    log_total = largest + jnp.log(totals)
    weights = jnp.where(live_keys, jnp.exp(scores - log_total[..., None]), 0.0)
    row_dots = lax.psum(jnp.sum(weights * weight_grad, -1), "seq")
    score_grad = (weights * (weight_grad - row_dots[..., None])).astype(jnp.bfloat16)
    weights_low = weights.astype(jnp.bfloat16)
    value_grad = jnp.einsum(
        "hqk,qhd->khd", weights_low, grad_heads, preferred_element_type=jnp.float32
    )
    value_grad = value_grad.astype(jnp.bfloat16).reshape(1, enc_rows, HEADS * HEAD_DIM)
    key_grad = jnp.einsum(
        "hqk,qhd->khd", score_grad, query_heads, preferred_element_type=jnp.float32
    )
    key_grad = key_grad.astype(jnp.bfloat16).reshape(1, enc_rows, HEADS * HEAD_DIM)
    local_sum = jnp.einsum(
        "hqk,khd->qhd", score_grad, key_heads, preferred_element_type=jnp.float32
    )
    local_sum = local_sum.reshape(dec_rows, HEADS * HEAD_DIM)
    query_grad = lax.psum_scatter(
        local_sum.astype(jnp.bfloat16), "seq", scatter_dimension=0, tiled=True
    )
    return (query_grad[None], key_grad, value_grad)


def solution(mesh):
    in_specs = (
        P("dp", "seq", None),
        P("dp", "seq", None),
        P("dp", "seq", None),
        P("dp", "seq", None),
        P("dp"),
    )
    out_specs = (P("dp", "seq", None), P("dp", "seq", None), P("dp", "seq", None))
    return jax.shard_map(body, mesh=mesh, in_specs=in_specs, out_specs=out_specs, check_vma=False)
```

profile of v0, /device:TPU:4, one launch (start us, length us, event | category | flops | bytes accessed | tf_op | source)
XLA Modules:
  0.0 716.1 jit_solution(12426405495881334180)
XLA Ops:
  7.2 0.0 all-gather.5.cloned.1.call-start
  7.2 0.7 all-gather.5.cloned.1.call-update
  7.9 0.0 all-gather.7.cloned.1.call-start
  7.9 0.7 all-gather.7.cloned.1.call-update
  8.6 0.0 reduce-scatter.2.cloned.1.call-start
  9.3 1.3 copy.48
  10.7 0.0 copy-start
  10.7 1.3 copy.49
  12.0 172.2 %all-gather.5.cloned.1.call-done = bf16[1,512,2048]{2,1,0:T(8,128)(2,1)} async-done(((bf16[1,16,2048]{2,1,0:T(8,128)(2,1)}), bf16[1,512,2048]{2,1,0:T(8,128)(2,1)}) %all-gather.5.cloned.1.call-update) | async-done | bytes 2097168 | tf_op jit(solution)/shard_map/all_gather | solution.py:32
  184.2 3.9 copy.28
  188.1 0.0 copy-done
  188.1 2.1 select_reduce_fusion.1
  190.3 84.2 %all-gather = f32[256,512]{1,0:T(8,128)S(1)} all-gather(f32[8,512]{1,0:T(8,128)S(1)} %get-tuple-element.156), channel_id=2, replica_groups=mesh['dp'=32,'seq'=32] {'seq'}, dimensions={0}, use_global_device_ids=true | all-gather | bytes 540672 | tf_op jit(solution)/shard_map/all_gather | solution.py:14
  274.4 0.5 select_reduce_fusion
  274.9 79.5 %all-gather.1 = f32[256,512]{1,0:T(8,128)S(1)} all-gather(f32[8,512]{1,0:T(8,128)S(1)} %select_reduce_fusion), channel_id=3, replica_groups=mesh['dp'=32,'seq'=32] {'seq'}, dimensions={0}, use_global_device_ids=true | all-gather | bytes 540672 | tf_op jit(solution)/shard_map/all_gather | solution.py:14
  354.5 0.0 copy-done.2
  354.5 0.8 copy-done.3
  355.3 24.1 %while.17 = (s32[]{:T(128)}, f32[8,512]{1,0:T(8,128)S(1)}, f32[8,512]{1,0:T(8,128)S(1)}, f32[32,8,512]{2,1,0:T(8,128)}, f32[32,8,512]{2,1,0:T(8,128)}, /*index=5*/s32[]{:T(128)}, s32[]{:T(128)}, s32[]{:T(128)}) while((s32[]{:T(128)}, f32[8,512]{1,0:T(8,128)S(1)}, f32[8,512]{1,0:T(8,128)S(1)}, f32[32,8,512]{2,1,0:T(8,128)}, ...), condition=%wide.region_3.4_spmd, body=%wide.region_2.3_spmd.sunk | while | flops 24581 | bytes 98427 | solution.py:19
  355.3 0.8 fusion.21
  356.0 0.8 fusion.21
  356.8 0.8 fusion.21
  357.6 0.8 fusion.21
  358.4 0.8 fusion.21
  359.1 0.8 fusion.21
  359.9 0.8 fusion.21
  360.7 0.8 fusion.21
  361.5 0.8 fusion.21
  362.3 0.8 fusion.21
  363.0 0.8 fusion.21
  363.8 0.8 fusion.21
  364.6 0.8 fusion.21
  365.4 0.8 fusion.21
  366.1 0.8 fusion.21
  366.9 0.8 fusion.21
  367.7 0.8 fusion.21
  368.5 0.8 fusion.21
  369.3 0.8 fusion.21
  370.0 0.8 fusion.21
  370.8 0.8 fusion.21
  371.6 0.8 fusion.21
  372.4 0.8 fusion.21
  373.1 0.8 fusion.21
  373.9 0.8 fusion.21
  374.7 0.8 fusion.21
  375.5 0.8 fusion.21
  376.3 0.8 fusion.21
  377.0 0.8 fusion.21
  377.8 0.8 fusion.21
  378.6 0.8 fusion.21
  379.4 0.0 all-gather.7.cloned.1.call-done
  379.4 3.9 copy.31
  383.3 3.5 multiply_reduce_fusion
  386.9 148.1 %psum.7 = f32[8,512]{1,0:T(8,128)S(1)} all-reduce(f32[8,512]{1,0:T(8,128)S(1)} %get-tuple-element.158), channel_id=1, replica_groups=mesh['dp'=32,'seq'=32] {'seq'}, use_global_device_ids=true, to_apply=%region_5.6 | all-reduce | flops 4096 | bytes 32768 | tf_op jit(solution)/shard_map/psum | solution.py:54
  535.0 2.4 multiply_convert_fusion
  537.4 2.0 convolution_convert_fusion
  539.5 4.0 copy.36
  543.4 0.0 reduce-scatter.2.cloned.1.call-update
  543.5 3.2 fusion.3
  546.7 1.3 copy.38
  548.0 1.0 copy.41
  549.0 2.4 fusion.4
  551.4 0.3 copy.40
  551.7 1.0 copy.42
  552.7 156.9 %reduce-scatter.2.cloned.1.call-done = bf16[16,2048]{1,0:T(8,128)(2,1)} async-done(((bf16[512,2048]{1,0:T(8,128)(2,1)}), bf16[16,2048]{1,0:T(8,128)(2,1)}) %reduce-scatter.2.cloned.1.call-update) | async-done | bytes 65552 | tf_op jit(solution)/shard_map/reduce_scatter | solution.py:69
  (8 shorter events, 0.0 us)
Async XLA Ops:
  7.2 177.0 %all-gather.5.cloned.1.call-start = ((), (), s32[]{:S(2)}) async-start(), calls=%async_computation.1 | async-start | bytes 2162688 | tf_op jit(solution)/shard_map/all_gather | solution.py:32
  7.9 371.5 %all-gather.7.cloned.1.call-start = ((), (), s32[]{:S(2)}) async-start(), calls=%async_computation.2 | async-start | bytes 2162688 | tf_op jit(solution)/shard_map/all_gather | solution.py:33
  8.6 700.9 %reduce-scatter.2.cloned.1.call-start = ((), (), s32[]{:S(2)}) async-start(), calls=%async_computation.3 | async-start | bytes 2162688 | tf_op jit(solution)/shard_map/reduce_scatter | solution.py:69
  10.7 177.5 %copy-start = (bf16[1,128,2048]{1,2,0:T(8,128)(2,1)}, bf16[1,128,2048]{1,2,0:T(8,128)(2,1)S(1)}, u32[]{:S(2)}) copy-start(bf16[1,128,2048]{1,2,0:T(8,128)(2,1)S(1)} %copy.48) | copy-start | bytes 1572868
  274.4 80.1 %copy-start.2 = (f32[256,512]{1,0:T(8,128)}, f32[256,512]{1,0:T(8,128)S(1)}, u32[]{:S(2)}) copy-start(f32[256,512]{1,0:T(8,128)S(1)} %all-gather) | copy-start | bytes 1572868
  354.5 0.8 copy-start.3
  535.0 2.4 copy-start.1
Sparse Core Ops, SparseCore 0:
  10.7 173.4 all-gather.4
  186.9 162.4 all-gather.6
  543.6 165.9 reduce-scatter.1
where the time goes:
time: 722 us; the launch traced here: 716 us
  waiting for transfers between devices  330 us (46%)
  blocking collectives  312 us (43%)
  other arithmetic  26.4 us (4%)
  local copies, waits for them, and re-layouts  18.9 us (3%)
  between operations  14.5 us (2%)
  matrix products  13.3 us (2%)
    all_gather x1, waiting for transfers between devices, body(): lax.all_gather(queries, 'seq', axis=1, tiled=True)  172 us
    all_gather x2, blocking collectives, joined(): gathered = jax.tree.map(lambda a: lax.all_gather(a, axis), part)  164 us
    reduce_scatter x1, waiting for transfers between devices, body(): lax.psum_scatter(local_sum.astype(jnp.bfloat16), 'seq', scatter_dimension...  157 us
    psum x1, blocking collectives, body(): row_dots = lax.psum(jnp.sum(weights * weight_grad, -1), 'seq')  148 us
    add x31, other arithmetic, combine_pair(): earlier[1] * jnp.exp(earlier[0] - largest)  23.5 us
  transfers between devices with their start and end apart: 3, of which 2 were waited for; matrix products, arithmetic and copies ran while one was open for 6% of the time, Pallas kernels for 0%

commit v1 on v0

v1 whole, which is shorter than its diff:
```python
import functools

import jax
import jax.numpy as jnp
from jax import lax
from jax.experimental import pallas as pl
from jax.experimental.pallas import tpu as pltpu
from jax.sharding import PartitionSpec as P

HEADS = 8
NZ = 8
NY = 4
MESH = pl.DeviceIdType.MESH
NEAR_FIRST = (1, 7, 2, 6, 3, 5, 4)
FAR_FIRST = (4, 3, 5, 2, 6, 1, 7)
DEAD = -1e30
FLOOR = -1e20


def nt(a, b):
    return lax.dot_general(a, b, (((1,), (1,)), ((), ())), preferred_element_type=jnp.float32)


def tn(a, b):
    return lax.dot_general(a, b, (((0,), (0,)), ((), ())), preferred_element_type=jnp.float32)


def kernel(
    len_ref, q_ref, k_ref, v_ref, g_ref,
    dq_ref, dk_ref, dv_ref,
    qb, gb, kb, vb, pb, wb, sb, dkb, dvb, dqb, dqr, dqz, mlo, mli, rdo, rdi,
    z_send, z_recv, y_send, y_recv, own,
):
    seq = lax.axis_index("seq")
    z, y = seq // NY, seq % NY
    enc, dim = kb.shape[1], kb.shape[2]
    rows = q_ref.shape[0]
    block = NZ * rows
    lanes = mlo.shape[1]
    dec = NY * block

    def zpeer(d):
        return ((z + d) % NZ) * NY + y

    def ypeer(e):
        return z * NY + (y + e) % NY

    def cols(head):
        return pl.ds(pl.multiple_of((head % NZ) * dim, dim), dim)

    def remote(src, dst, send, recv, peer):
        return pltpu.make_async_remote_copy(
            src_ref=src, dst_ref=dst, send_sem=send, recv_sem=recv,
            device_id={"seq": peer}, device_id_type=MESH,
        )

    started = []

    def go(copy):
        copy.start()
        started.append(copy)
        return copy

    here = [
        pltpu.make_async_copy(q_ref.at[:, cols(z)], qb.at[pl.ds(0, rows)], own.at[0]),
        pltpu.make_async_copy(g_ref.at[:, cols(z)], gb.at[pl.ds(0, rows)], own.at[1]),
        pltpu.make_async_copy(k_ref.at[:, cols(z)], kb.at[0], own.at[2]),
        pltpu.make_async_copy(v_ref.at[:, cols(z)], vb.at[0], own.at[3]),
    ]
    for copy in here:
        copy.start()

    barrier = pltpu.get_barrier_semaphore()
    for d in range(1, NZ):
        pl.semaphore_signal(barrier, inc=1, device_id={"seq": zpeer(d)}, device_id_type=MESH)
    for e in range(1, NY):
        pl.semaphore_signal(barrier, inc=1, device_id={"seq": ypeer(e)}, device_id_type=MESH)
    pl.semaphore_wait(barrier, NZ - 1 + NY - 1)

    def z_out(kind, src, dst_at, order):
        return {
            d: go(remote(src.at[:, cols(z + d)], dst_at(d), z_send.at[kind, d], z_recv.at[kind, d], zpeer(d)))
            for d in order
        }

    q_in = z_out(0, q_ref, lambda d: qb.at[pl.ds(d * rows, rows)], FAR_FIRST)
    g_in = z_out(1, g_ref, lambda d: gb.at[pl.ds(d * rows, rows)], FAR_FIRST)
    k_in = z_out(2, k_ref, lambda d: kb.at[d], FAR_FIRST)

    def y_out(kind, buf):
        return {
            e: go(remote(
                buf.at[pl.ds(0, block)], buf.at[pl.ds(e * block, block)],
                y_send.at[kind, e], y_recv.at[kind, e], ypeer(e),
            ))
            for e in range(1, NY)
        }

    here[0].wait()
    for d in NEAR_FIRST:
        q_in[d].wait_recv()
    q_all = y_out(0, qb)
    here[1].wait()
    for d in NEAR_FIRST:
        g_in[d].wait_recv()
    g_all = y_out(1, gb)
    v_in = z_out(3, v_ref, lambda d: vb.at[d], FAR_FIRST)

    for e in range(1, NY):
        q_all[e].wait_recv()

    length = len_ref[0]
    tops, sums = [None] * NZ, [None] * NZ
    for d in (0,) + NEAR_FIRST:
        if d == 0:
            here[2].wait()
        else:
            k_in[d].wait_recv()
        scores = nt(kb[d], qb[...])
        base = (((z - d + NZ) % NZ) * NY + y) * enc
        live = base + lax.broadcasted_iota(jnp.int32, (enc, dec), 0) < length
        scores = jnp.where(live, scores, DEAD)
        top = jnp.maximum(jnp.max(scores, axis=0, keepdims=True), FLOOR)
        powers = jnp.exp(scores - top)
        tops[d], sums[d] = top, jnp.sum(powers, axis=0, keepdims=True)
        pb[d] = powers

    top = functools.reduce(jnp.maximum, tops)
    total = functools.reduce(jnp.add, [s * jnp.exp(t - top) for s, t in zip(sums, tops)])
    for i in range(NY):
        mlo[i : i + 1, :] = top[:, i * lanes : (i + 1) * lanes]
        mlo[NY + i : NY + i + 1, :] = total[:, i * lanes : (i + 1) * lanes]

    ml = {
        e: go(remote(mlo, mli.at[e], y_send.at[2, e], y_recv.at[2, e], ypeer(e)))
        for e in range(1, NY)
    }

    def arrived(buf, e, first):
        at = [first + (i - e) % NY for i in range(NY)]
        return jnp.concatenate([buf[e, r : r + 1, :] for r in at], axis=1)

    for e in range(1, NY):
        g_all[e].wait_recv()
    for e in range(1, NY):
        ml[e].wait_recv()
    all_tops = [top] + [arrived(mli, e, 0) for e in range(1, NY)]
    all_sums = [total] + [arrived(mli, e, NY) for e in range(1, NY)]
    largest = functools.reduce(jnp.maximum, all_tops)
    total = functools.reduce(jnp.add, [s * jnp.exp(t - largest) for s, t in zip(all_sums, all_tops)])
    share = 1.0 / total

    def z_back(kind, d, src, dst):
        return go(remote(
            src, dst.at[:, cols(z)], z_send.at[kind, d], z_recv.at[kind, d], zpeer(NZ - d),
        ))

    dv_in, dk_in, dq_in = {}, {}, {}
    for d in FAR_FIRST + (0,):
        weights = pb[d] * (jnp.exp(tops[d] - largest) * share)
        pb[d] = weights
        grad = jnp.dot(weights.astype(jnp.bfloat16), gb[...], preferred_element_type=jnp.float32)
        dvb[d] = grad.astype(jnp.bfloat16)
        if d:
            dv_in[d] = z_back(4, d, dvb.at[d], dv_ref)
    dv_own = pltpu.make_async_copy(dvb.at[0], dv_ref.at[:, cols(z)], own.at[4])
    dv_own.start()

    dots = jnp.zeros((1, dec), jnp.float32)
    for d in (0,) + NEAR_FIRST:
        if d == 0:
            here[3].wait()
        else:
            v_in[d].wait_recv()
        weight_grad = nt(vb[d], gb[...])
        wb[d] = weight_grad
        dots = dots + jnp.sum(pb[d] * weight_grad, axis=0, keepdims=True)
    rdo[...] = jnp.zeros_like(rdo)
    for i in range(NY):
        rdo[i : i + 1, :] = dots[:, i * lanes : (i + 1) * lanes]
    rd = {
        e: go(remote(rdo, rdi.at[e], y_send.at[3, e], y_recv.at[3, e], ypeer(e)))
        for e in range(1, NY)
    }
    for e in range(1, NY):
        rd[e].wait_recv()
    for e in range(1, NY):
        dots = dots + arrived(rdi, e, 0)

    for d in range(NZ):
        sb[pl.ds(d * enc, enc), :] = (pb[d] * (wb[d] - dots)).astype(jnp.bfloat16)

    keys = kb[...].reshape(NZ * enc, dim)
    dq_y = {}
    for e in range(1, NY):
        part = tn(sb[:, e * block : (e + 1) * block], keys)
        dqb[e] = part.astype(jnp.bfloat16)
        dq_y[e] = go(remote(dqb.at[e], dqr.at[e], y_send.at[4, e], y_recv.at[4, e], ypeer(NY - e)))
    mine = tn(sb[:, 0:block], keys)

    for d in FAR_FIRST + (0,):
        grad = jnp.dot(sb[pl.ds(d * enc, enc), :], qb[...], preferred_element_type=jnp.float32)
        dkb[d] = grad.astype(jnp.bfloat16)
        if d:
            dk_in[d] = z_back(5, d, dkb.at[d], dk_ref)
    dk_own = pltpu.make_async_copy(dkb.at[0], dk_ref.at[:, cols(z)], own.at[5])
    dk_own.start()

    for e in range(1, NY):
        dq_y[e].wait_recv()
        mine = mine + dqr[e].astype(jnp.float32)
    dqz[...] = mine.astype(jnp.bfloat16)
    for d in FAR_FIRST:
        dq_in[d] = z_back(6, d, dqz.at[pl.ds(d * rows, rows)], dq_ref)
    dq_own = pltpu.make_async_copy(dqz.at[pl.ds(0, rows)], dq_ref.at[:, cols(z)], own.at[6])
    dq_own.start()

    for copy in (dv_own, dk_own, dq_own):
        copy.wait()
    for group in (dv_in, dk_in, dq_in):
        for d in NEAR_FIRST:
            group[d].wait_recv()
    for copy in started:
        copy.wait_send()


def body(queries, enc_keys, enc_values, grad_context, enc_lengths):
    rows, width = queries.shape[1:]
    enc = enc_keys.shape[1]
    dim = width // HEADS
    block = NZ * rows
    dec = NY * block
    any_spec = pl.BlockSpec(memory_space=pl.ANY)
    bf16, f32 = jnp.bfloat16, jnp.float32
    dq, dk, dv = pl.pallas_call(
        kernel,
        out_shape=(
            jax.ShapeDtypeStruct((rows, width), bf16),
            jax.ShapeDtypeStruct((enc, width), bf16),
            jax.ShapeDtypeStruct((enc, width), bf16),
        ),
        in_specs=[pl.BlockSpec(memory_space=pltpu.SMEM)] + [any_spec] * 4,
        out_specs=(any_spec,) * 3,
        scratch_shapes=[
            pltpu.VMEM((dec, dim), bf16),
            pltpu.VMEM((dec, dim), bf16),
            pltpu.VMEM((NZ, enc, dim), bf16),
            pltpu.VMEM((NZ, enc, dim), bf16),
            pltpu.VMEM((NZ, enc, dec), f32),
            pltpu.VMEM((NZ, enc, dec), f32),
            pltpu.VMEM((NZ * enc, dec), bf16),
            pltpu.VMEM((NZ, enc, dim), bf16),
            pltpu.VMEM((NZ, enc, dim), bf16),
            pltpu.VMEM((NY, block, dim), bf16),
            pltpu.VMEM((NY, block, dim), bf16),
            pltpu.VMEM((block, dim), bf16),
            pltpu.VMEM((2 * NY, dec // NY), f32),
            pltpu.VMEM((NY, 2 * NY, dec // NY), f32),
            pltpu.VMEM((2 * NY, dec // NY), f32),
            pltpu.VMEM((NY, 2 * NY, dec // NY), f32),
            pltpu.SemaphoreType.DMA((7, NZ)),
            pltpu.SemaphoreType.DMA((7, NZ)),
            pltpu.SemaphoreType.DMA((5, NY)),
            pltpu.SemaphoreType.DMA((5, NY)),
            pltpu.SemaphoreType.DMA((7,)),
        ],
        compiler_params=pltpu.CompilerParams(
            collective_id=0, has_side_effects=True, vmem_limit_bytes=32 * 1024 * 1024
        ),
        cost_estimate=pl.CostEstimate(
            flops=10 * NZ * enc * dec * dim,
            bytes_accessed=8 * enc * width + 6 * rows * width,
            transcendentals=NZ * enc * dec,
        ),
    )(enc_lengths, queries[0], enc_keys[0], enc_values[0], grad_context[0])
    return (dq[None], dk[None], dv[None])


def solution(mesh):
    spec = P("dp", "seq", None)
    return jax.shard_map(
        body,
        mesh=mesh,
        in_specs=(spec, spec, spec, spec, P("dp")),
        out_specs=(spec, spec, spec),
        check_vma=False,
    )
```

time: 722 us -> 78.5 us (0.11)
  the two profiles are of different devices: /device:TPU:4 before, /device:TPU:112 now
where the time goes in v1:
time: 78.5 us; the launch traced here: 77.7 us
  Pallas kernels  70.4 us (90%)
  local copies, waits for them, and re-layouts  5.97 us (8%)
  between operations  1.3 us (2%)
    pallas_call x1, Pallas kernels, body(): pl.pallas_call(kernel, out_shape=(jax.ShapeDtypeStruct((rows, width), bf1...  70.4 us
    unnamed x11, local copies, waits for them, and re-layouts  5.97 us

profile of v1, /device:TPU:112, one launch (start us, length us, event | category | flops | bytes accessed | tf_op | source)
XLA Modules:
  0.0 77.7 jit_solution(9262719430280888358)
XLA Ops:
  1.3 0.0 copy-start
  1.3 1.0 %copy-done = bf16[1,128,2048]{2,1,0:T(8,128)(2,1)S(1)} copy-done((bf16[1,128,2048]{2,1,0:T(8,128)(2,1)S(1)}, bf16[1,128,2048]{2,1,0:T(8,128)(2,1)}, u32[]{:S(2)}) %copy-start) | copy-done | bytes 524312
  2.3 0.0 copy-start.1
  2.3 1.0 %copy-done.1 = bf16[1,128,2048]{2,1,0:T(8,128)(2,1)S(1)} copy-done((bf16[1,128,2048]{2,1,0:T(8,128)(2,1)S(1)}, bf16[1,128,2048]{2,1,0:T(8,128)(2,1)}, u32[]{:S(2)}) %copy-start.1) | copy-done | bytes 524312
  3.4 0.0 copy-start.2
  3.4 0.8 %copy-done.2 = bf16[1,16,2048]{2,1,0:T(8,128)(2,1)S(1)} copy-done((bf16[1,16,2048]{2,1,0:T(8,128)(2,1)S(1)}, bf16[1,16,2048]{2,1,0:T(8,128)(2,1)}, u32[]{:S(2)}) %copy-start.2) | copy-done | bytes 65560
  4.2 0.0 copy-start.3
  4.2 0.8 %copy-done.3 = bf16[1,16,2048]{2,1,0:T(8,128)(2,1)S(1)} copy-done((bf16[1,16,2048]{2,1,0:T(8,128)(2,1)S(1)}, bf16[1,16,2048]{2,1,0:T(8,128)(2,1)}, u32[]{:S(2)}) %copy-start.3) | copy-done | bytes 65560
  5.0 70.4 %shard_map.76 = (bf16[16,2048]{1,0:T(8,128)(2,1)S(1)}, bf16[128,2048]{1,0:T(8,128)(2,1)S(1)}, bf16[128,2048]{1,0:T(8,128)(2,1)S(1)}) custom-call(s32[1]{0:T(128)S(6)} %copy.11.len_ref, bf16[16,2048]{1,0:T(8,128)(2,1)S(1)} %bitcast.12, bf16[128,2048]{1,0:T(8,128)(2,1)S(1)} %bitcast.10, bf16[128,2048]{1,0:T(8,128)(2,1)S(1)} %bitcast.11, ...), custom_call_target="tpu_custom_call" | custom-call | flops 1342177280 | bytes 2293760 | tf_op jit(solution)/shard_map/pallas_call | solution.py:235
  75.4 0.6 copy.12
  76.1 0.8 %copy.13 = bf16[1,128,2048]{2,1,0:T(8,128)(2,1)} copy(bf16[1,128,2048]{2,1,0:T(8,128)(2,1)S(1)} %bitcast.8) | data formatting | bytes 1048576
  76.9 0.8 %copy.14 = bf16[1,128,2048]{2,1,0:T(8,128)(2,1)} copy(bf16[1,128,2048]{2,1,0:T(8,128)(2,1)S(1)} %bitcast.7) | data formatting | bytes 1048576
Async XLA Ops:
  1.3 1.0 %copy-start = (bf16[1,128,2048]{2,1,0:T(8,128)(2,1)S(1)}, bf16[1,128,2048]{2,1,0:T(8,128)(2,1)}, u32[]{:S(2)}) copy-start(bf16[1,128,2048]{2,1,0:T(8,128)(2,1)} %param.6) | copy-start | bytes 1572868
  2.3 1.0 %copy-start.1 = (bf16[1,128,2048]{2,1,0:T(8,128)(2,1)S(1)}, bf16[1,128,2048]{2,1,0:T(8,128)(2,1)}, u32[]{:S(2)}) copy-start(bf16[1,128,2048]{2,1,0:T(8,128)(2,1)} %param.7) | copy-start | bytes 1572868
  3.4 0.8 %copy-start.2 = (bf16[1,16,2048]{2,1,0:T(8,128)(2,1)S(1)}, bf16[1,16,2048]{2,1,0:T(8,128)(2,1)}, u32[]{:S(2)}) copy-start(bf16[1,16,2048]{2,1,0:T(8,128)(2,1)} %param.5) | copy-start | bytes 196612
  4.2 0.8 %copy-start.3 = (bf16[1,16,2048]{2,1,0:T(8,128)(2,1)S(1)}, bf16[1,16,2048]{2,1,0:T(8,128)(2,1)}, u32[]{:S(2)}) copy-start(bf16[1,16,2048]{2,1,0:T(8,128)(2,1)} %param.8) | copy-start | bytes 196612

commit v2 on v0

v2 whole, which is shorter than its diff:
```python
import functools

import jax
import jax.numpy as jnp
from jax import lax
from jax.experimental import pallas as pl
from jax.experimental.pallas import tpu as pltpu
from jax.sharding import PartitionSpec as P

HEADS = 8
NZ = 8
NY = 4
GZ = 4
MESH = pl.DeviceIdType.MESH
DEAD = -1e30
FLOOR = -1e20
PIECES = ((2, 1), (-2, 1), (1, 1), (-1, 1), (2, 0), (-2, 0), (1, 0), (-1, 0), (0, 1))
CHUNK = {0: 0, 1: 1, -1: 2, 2: 3, -2: 3}
NEAR = (4, 3, 5, 2, 6, 1, 7)


def nt(a, b):
    return lax.dot_general(a, b, (((1,), (1,)), ((), ())), preferred_element_type=jnp.float32)


def tn(a, b):
    return lax.dot_general(a, b, (((0,), (0,)), ((), ())), preferred_element_type=jnp.float32)


def kernel(
    len_ref, q_hbm, k_hbm, v_hbm, g_hbm,
    dq_ref, dk_ref, dv_ref,
    q_ref, k_ref, v_ref, g_ref, dqo, dko, dvo,
    qz, gz, qb, gb, kb, vb, pb, wb, sb, dkb, dvb, dqb, dqy, dqz, dqr, mlo, mli, rdo, rdi,
    z_send, z_recv, y_send, y_recv, p_send, p_recv, s_send, s_recv, own,
):
    seq = lax.axis_index("seq")
    z, y = seq // NY, seq % NY
    rows = q_ref.shape[0]
    enc = k_ref.shape[0]
    dim = kb.shape[2]
    block = NZ * rows
    dec = NY * block
    lanes = mlo.shape[1]
    half = enc // 2
    side = y % 2
    other = y + 1 - 2 * side

    def device(dz, at_y):
        return ((z + dz + NZ) % NZ) * NY + at_y

    def zpeer(d):
        return device(d, y)

    def ypeer(e):
        return z * NY + (y + e) % NY

    def cols(dz, at_y):
        head = 2 * ((z + dz + NZ) % GZ) + at_y % 2
        return pl.ds(pl.multiple_of(head * dim, dim), dim)

    def pair(dz):
        return pl.ds(pl.multiple_of(((z + dz + NZ) % GZ) * (2 * dim), 2 * dim), 2 * dim)

    def half_of(at_y):
        return pl.ds(pl.multiple_of((at_y % 2) * dim, dim), dim)

    def part(dz):
        return {2: pl.ds(0, half), -2: pl.ds(half, half)}.get(dz, pl.ds(0, enc))

    def remote(src, dst, send, recv, peer):
        return pltpu.make_async_remote_copy(
            src_ref=src, dst_ref=dst, send_sem=send, recv_sem=recv,
            device_id={"seq": peer}, device_id_type=MESH,
        )

    started = []

    def go(copy):
        copy.start()
        started.append(copy)
        return copy

    loads = [
        pltpu.make_async_copy(src, dst, own.at[i])
        for i, (src, dst) in enumerate(((q_hbm, q_ref), (g_hbm, g_ref), (k_hbm, k_ref), (v_hbm, v_ref)))
    ]
    for copy in loads:
        copy.start()

    barrier = pltpu.get_barrier_semaphore()
    peers = [zpeer(d) for d in range(1, NZ)] + [ypeer(e) for e in range(1, NY)]
    peers += [device(dz, other) for dz in (1, -1, 2, -2)] + [device(4, (y + 2) % NY)]
    for peer in peers:
        pl.semaphore_signal(barrier, inc=1, device_id={"seq": peer}, device_id_type=MESH)
    pl.semaphore_wait(barrier, len(peers))

    def z_out(kind, src, into):
        return {
            d: go(remote(
                src.at[:, pair(d)], into.at[pl.ds(d * rows, rows)], z_send.at[kind, d], z_recv.at[kind, d], zpeer(d),
            ))
            for d in NEAR
        }

    def y_out(kind, src, into):
        return {
            e: go(remote(
                src.at[:, half_of(y + e)], into.at[pl.ds(e * block, block)],
                y_send.at[kind, e], y_recv.at[kind, e], ypeer(e),
            ))
            for e in (2, 3, 1)
        }

    def p_out(kind, src, into):
        out = {}
        for i, (dz, turn) in enumerate(PIECES):
            at_y = other if turn else y
            at = into.at[4 * turn + CHUNK[dz], part(dz)] if dz in (2, -2) else into.at[4 * turn + CHUNK[dz]]
            out[dz, turn] = go(remote(
                src.at[part(dz), cols(dz, at_y)], at, p_send.at[kind, i], p_recv.at[kind, i], device(dz, at_y),
            ))
        return out

    loads[0].wait()
    q_in = z_out(0, q_ref, qz)
    loads[1].wait()
    g_in = z_out(1, g_ref, gz)
    loads[2].wait()
    k_in = p_out(0, k_ref, kb)
    loads[3].wait()

    qz[0:rows, :] = q_ref[:, pair(0)]
    gz[0:rows, :] = g_ref[:, pair(0)]
    for d in reversed(NEAR):
        q_in[d].wait_recv()
    q_all = y_out(0, qz, qb)
    for d in reversed(NEAR):
        g_in[d].wait_recv()
    g_all = y_out(1, gz, gb)
    v_in = p_out(1, v_ref, vb)

    qb[0:block, :] = qz[:, half_of(y)]
    gb[0:block, :] = gz[:, half_of(y)]
    kb[0] = k_ref[:, cols(0, y)]
    vb[0] = v_ref[:, cols(0, y)]
    for e in range(1, NY):
        q_all[e].wait_recv()

    def arrive(copies, c):
        turn, i = divmod(c, 4)
        for dz in ((0,), (1,), (-1,), (2, -2))[i]:
            if (dz, turn) in copies:
                copies[dz, turn].wait_recv()

    order = (0, 4, 1, 2, 5, 6, 3, 7)

    length = len_ref[0]
    row = lax.broadcasted_iota(jnp.int32, (enc, dec), 0)
    tops, sums = [None] * 8, [None] * 8
    for c in order:
        arrive(k_in, c)
        turn, i = divmod(c, 4)
        at_y = other if turn else y

        def base(dz):
            return (((z + dz + NZ) % NZ) * NY + at_y) * enc

        first = (0, -1, 1, -2)[i]
        live = row + base(first) < length
        if i == 3:
            live = jnp.where(row < half, row + base(-2), row + base(2)) < length
        scores = jnp.where(live, nt(kb[c], qb[...]), DEAD)
        top = jnp.maximum(jnp.max(scores, axis=0, keepdims=True), FLOOR)
        powers = jnp.exp(scores - top)
        tops[c], sums[c] = top, jnp.sum(powers, axis=0, keepdims=True)
        pb[c] = powers

    shared = (device(4, y), device(0, (y + 2) % NY), device(4, (y + 2) % NY))
    turned = ((4, 0), (0, 2), (4, 2))

    def put(buf, at, values):
        for i in range(NY):
            buf[at + i : at + i + 1, :] = values[:, i * lanes : (i + 1) * lanes]

    def exchange(kind, out, into):
        return [
            go(remote(out, into.at[i], s_send.at[kind, i], s_recv.at[kind, i], shared[i]))
            for i in range(3)
        ]

    def take(buf, i, at):
        tile = buf[i]
        if turned[i][0]:
            tile = pltpu.roll(tile, lanes // 2, 1)
        return jnp.concatenate(
            [tile[at + (k + turned[i][1]) % NY : at + (k + turned[i][1]) % NY + 1, :] for k in range(NY)], axis=1
        )

    top = functools.reduce(jnp.maximum, tops)
    total = functools.reduce(jnp.add, [s * jnp.exp(t - top) for s, t in zip(sums, tops)])
    put(mlo, 0, top)
    put(mlo, NY, total)
    ml = exchange(0, mlo, mli)
    for e in range(1, NY):
        g_all[e].wait_recv()
    for copy in ml:
        copy.wait_recv()
    all_tops = [top] + [take(mli, i, 0) for i in range(3)]
    all_sums = [total] + [take(mli, i, NY) for i in range(3)]
    largest = functools.reduce(jnp.maximum, all_tops)
    total = functools.reduce(jnp.add, [s * jnp.exp(t - largest) for s, t in zip(all_sums, all_tops)])
    share = 1.0 / total

    dots = jnp.zeros((1, dec), jnp.float32)
    for c in order:
        arrive(v_in, c)
        weights = pb[c] * (jnp.exp(tops[c] - largest) * share)
        pb[c] = weights
        weight_grad = nt(vb[c], gb[...])
        wb[c] = weight_grad
        dots = dots + jnp.sum(weights * weight_grad, axis=0, keepdims=True)
    rdo[...] = jnp.zeros_like(rdo)
    put(rdo, 0, dots)
    rd = exchange(1, rdo, rdi)

    def give(kind, src, into, c):
        turn, i = divmod(c, 4)
        out = {}
        for dz in ((0,), (1,), (-1,), (2, -2))[i]:
            if (dz, turn) not in PIECES:
                into[:, cols(0, y)] = src[c]
                continue
            at_y = other if turn else y
            at = src.at[c, part(dz)] if dz in (2, -2) else src.at[c]
            n = PIECES.index((dz, turn))
            out[dz, turn] = go(remote(
                at, into.at[part(dz), cols(0, y)], p_send.at[kind, n], p_recv.at[kind, n], device(-dz, at_y),
            ))
        return out

    back = {2: {}, 3: {}}
    far_first = (7, 3, 5, 6, 1, 2, 4, 0)
    for c in far_first:
        grad = jnp.dot(pb[c].astype(jnp.bfloat16), gb[...], preferred_element_type=jnp.float32)
        dvb[c] = grad.astype(jnp.bfloat16)
        back[2].update(give(2, dvb, dvo, c))

    for copy in rd:
        copy.wait_recv()
    for i in range(3):
        dots = dots + take(rdi, i, 0)
    for c in range(8):
        sb[pl.ds(c * enc, enc), :] = (pb[c] * (wb[c] - dots)).astype(jnp.bfloat16)

    keys = kb[...].reshape(8 * enc, dim)
    dq_y = {}
    for e in (2, 3, 1):
        dqb[e] = tn(sb[:, e * block : (e + 1) * block], keys).astype(jnp.bfloat16)
        dq_y[e] = go(remote(dqb.at[e], dqy.at[e], y_send.at[2, e], y_recv.at[2, e], ypeer(NY - e)))
    mine = tn(sb[:, 0:block], keys)

    for c in far_first:
        grad = jnp.dot(sb[pl.ds(c * enc, enc), :], qb[...], preferred_element_type=jnp.float32)
        dkb[c] = grad.astype(jnp.bfloat16)
        back[3].update(give(3, dkb, dko, c))

    for e in range(1, NY):
        dq_y[e].wait_recv()
    mine = (mine + dqy[2].astype(jnp.float32)).astype(jnp.bfloat16)
    theirs = (dqy[1].astype(jnp.float32) + dqy[3].astype(jnp.float32)).astype(jnp.bfloat16)
    dqz[:, half_of(y)] = mine
    dqz[:, half_of(other)] = theirs
    dq_z = {
        d: go(remote(
            dqz.at[pl.ds(d * rows, rows)], dqr.at[d], z_send.at[2, d], z_recv.at[2, d], zpeer(NZ - d),
        ))
        for d in NEAR
    }
    dqr[0] = dqz[0:rows, :]

    for copy in back[2].values():
        copy.wait_recv()
    out_v = pltpu.make_async_copy(dvo, dv_ref, own.at[4])
    out_v.start()
    for copy in back[3].values():
        copy.wait_recv()
    out_k = pltpu.make_async_copy(dko, dk_ref, own.at[5])
    out_k.start()
    for d in range(1, NZ):
        dq_z[d].wait_recv()
    for d in range(GZ):
        dqo[:, pair(d)] = (dqr[d].astype(jnp.float32) + dqr[d + GZ].astype(jnp.float32)).astype(jnp.bfloat16)
    out_q = pltpu.make_async_copy(dqo, dq_ref, own.at[6])
    out_q.start()
    for copy in started:
        copy.wait_send()
    for copy in (out_v, out_k, out_q):
        copy.wait()


def settle(dq_from, dk_from, dv_from, dq_ref, dk_ref, dv_ref):
    dq_ref[...] = dq_from[...]
    dk_ref[...] = dk_from[...]
    dv_ref[...] = dv_from[...]


def body(queries, enc_keys, enc_values, grad_context, enc_lengths):
    rows, width = queries.shape[1:]
    enc = enc_keys.shape[1]
    dim = width // HEADS
    block = NZ * rows
    dec = NY * block
    lanes = dec // NY
    any_spec = pl.BlockSpec(memory_space=pl.ANY)
    bf16, f32 = jnp.bfloat16, jnp.float32
    vmem = pltpu.VMEM
    dma = pltpu.SemaphoreType.DMA
    outs = (
        jax.ShapeDtypeStruct((rows, width), bf16),
        jax.ShapeDtypeStruct((enc, width), bf16),
        jax.ShapeDtypeStruct((enc, width), bf16),
    )
    grads = pl.pallas_call(
        kernel,
        out_shape=outs,
        in_specs=[pl.BlockSpec(memory_space=pltpu.SMEM)] + [any_spec] * 4,
        out_specs=(any_spec,) * 3,
        scratch_shapes=[
            vmem((rows, width), bf16), vmem((enc, width), bf16),
            vmem((enc, width), bf16), vmem((rows, width), bf16),
            vmem((rows, width), bf16), vmem((enc, width), bf16), vmem((enc, width), bf16),
            vmem((block, 2 * dim), bf16), vmem((block, 2 * dim), bf16),
            vmem((dec, dim), bf16), vmem((dec, dim), bf16),
            vmem((8, enc, dim), bf16), vmem((8, enc, dim), bf16),
            vmem((8, enc, dec), f32), vmem((8, enc, dec), f32),
            vmem((8 * enc, dec), bf16),
            vmem((8, enc, dim), bf16), vmem((8, enc, dim), bf16),
            vmem((NY, block, dim), bf16), vmem((NY, block, dim), bf16),
            vmem((block, 2 * dim), bf16), vmem((NZ, rows, 2 * dim), bf16),
            vmem((2 * NY, lanes), f32), vmem((3, 2 * NY, lanes), f32),
            vmem((2 * NY, lanes), f32), vmem((3, 2 * NY, lanes), f32),
            dma((3, NZ)), dma((3, NZ)), dma((3, NY)), dma((3, NY)),
            dma((4, len(PIECES))), dma((4, len(PIECES))), dma((2, 3)), dma((2, 3)), dma((7,)),
        ],
        compiler_params=pltpu.CompilerParams(
            collective_id=0, has_side_effects=True, vmem_limit_bytes=56 * 1024 * 1024
        ),
        cost_estimate=pl.CostEstimate(
            flops=80 * enc * dec * dim,
            bytes_accessed=8 * enc * width + 6 * rows * width,
            transcendentals=8 * enc * dec,
        ),
    )(enc_lengths, queries[0], enc_keys[0], enc_values[0], grad_context[0])
    parts = 1
    specs = tuple(pl.BlockSpec((a.shape[0] // parts, width), lambda i: (i, 0)) for a in outs)
    dq, dk, dv = pl.pallas_call(settle, grid=(parts,), out_shape=outs, in_specs=specs, out_specs=specs)(*grads)
    return (dq[None], dk[None], dv[None])


def solution(mesh):
    spec = P("dp", "seq", None)
    return jax.shard_map(
        body,
        mesh=mesh,
        in_specs=(spec, spec, spec, spec, P("dp")),
        out_specs=(spec, spec, spec),
        check_vma=False,
    )
```

time: 722 us -> 71.9 us (0.10)
  the two profiles are of different devices: /device:TPU:4 before, /device:TPU:112 now
where the time goes in v2:
time: 71.9 us; the launch traced here: 71.7 us
  Pallas kernels  70.4 us (98%)
  between operations  1.29 us (2%)
    pallas_call x1, Pallas kernels, body(): pl.pallas_call(kernel, out_shape=outs, in_specs=[pl.BlockSpec(memory_spac...  68.2 us
    pallas_call x1, Pallas kernels, body(): pl.pallas_call(settle, grid=(parts,), out_shape=outs, in_specs=specs, out...  2.24 us

profile of v2, /device:TPU:112, one launch (start us, length us, event | category | flops | bytes accessed | tf_op | source)
XLA Modules:
  0.0 71.7 jit_solution(2583628648692222439)
XLA Ops:
  1.3 68.2 %shard_map.76 = (bf16[16,2048]{1,0:T(8,128)(2,1)}, bf16[128,2048]{1,0:T(8,128)(2,1)}, bf16[128,2048]{1,0:T(8,128)(2,1)}) custom-call(s32[1]{0:T(128)S(6)} %copy.8.len_ref, bf16[16,2048]{1,0:T(8,128)(2,1)} %bitcast.11, bf16[128,2048]{1,0:T(8,128)(2,1)} %bitcast.7, bf16[128,2048]{1,0:T(8,128)(2,1)} %bitcast.8, bf16[16,2048]{1,0:T(8,128)(2,1)} %bitcast.12), custom_call_target="tpu_custom_call" | custom-call | flops 1342177280 | bytes 2293760 | tf_op jit(solution)/shard_map/pallas_call | solution.py:324
  69.5 2.2 %shard_map.77 = (bf16[16,2048]{1,0:T(8,128)(2,1)}, bf16[128,2048]{1,0:T(8,128)(2,1)}, bf16[128,2048]{1,0:T(8,128)(2,1)}) custom-call(bf16[16,2048]{1,0:T(8,128)(2,1)} %get-tuple-element.9.dq_from, bf16[128,2048]{1,0:T(8,128)(2,1)} %get-tuple-element.10.dk_from, bf16[128,2048]{1,0:T(8,128)(2,1)} %get-tuple-element.11.dv_from), custom_call_target="tpu_custom_call" | custom-call | tf_op jit(solution)/shard_map/pallas_call | solution.py:357

commit v3 on v2

--- a/solution.py
+++ b/solution.py
@@ -204,25 +204,24 @@
     ml = exchange(0, mlo, mli)
     for e in range(1, NY):
         g_all[e].wait_recv()
+
+    dots = jnp.zeros((1, dec), jnp.float32)
+    for c in order:
+        arrive(v_in, c)
+        weight_grad = nt(vb[c], gb[...])
+        wb[c] = weight_grad
+        dots = dots + jnp.sum(pb[c] * weight_grad, axis=0, keepdims=True) * jnp.exp(tops[c] - top)
+    rdo[...] = jnp.zeros_like(rdo)
+    put(rdo, 0, dots)
+    rd = exchange(1, rdo, rdi)
+
     for copy in ml:
         copy.wait_recv()
     all_tops = [top] + [take(mli, i, 0) for i in range(3)]
     all_sums = [total] + [take(mli, i, NY) for i in range(3)]
     largest = functools.reduce(jnp.maximum, all_tops)
-    total = functools.reduce(jnp.add, [s * jnp.exp(t - largest) for s, t in zip(all_sums, all_tops)])
-    share = 1.0 / total
-
-    dots = jnp.zeros((1, dec), jnp.float32)
-    for c in order:
-        arrive(v_in, c)
-        weights = pb[c] * (jnp.exp(tops[c] - largest) * share)
-        pb[c] = weights
-        weight_grad = nt(vb[c], gb[...])
-        wb[c] = weight_grad
-        dots = dots + jnp.sum(weights * weight_grad, axis=0, keepdims=True)
-    rdo[...] = jnp.zeros_like(rdo)
-    put(rdo, 0, dots)
-    rd = exchange(1, rdo, rdi)
+    scales = [jnp.exp(t - largest) for t in all_tops]
+    share = 1.0 / functools.reduce(jnp.add, [s * r for s, r in zip(all_sums, scales)])
 
     def give(kind, src, into, c):
         turn, i = divmod(c, 4)
@@ -242,14 +241,16 @@
     back = {2: {}, 3: {}}
     far_first = (7, 3, 5, 6, 1, 2, 4, 0)
     for c in far_first:
-        grad = jnp.dot(pb[c].astype(jnp.bfloat16), gb[...], preferred_element_type=jnp.float32)
+        weights = pb[c] * (jnp.exp(tops[c] - largest) * share)
+        pb[c] = weights
+        grad = jnp.dot(weights.astype(jnp.bfloat16), gb[...], preferred_element_type=jnp.float32)
         dvb[c] = grad.astype(jnp.bfloat16)
         back[2].update(give(2, dvb, dvo, c))
 
     for copy in rd:
         copy.wait_recv()
-    for i in range(3):
-        dots = dots + take(rdi, i, 0)
+    all_dots = [dots] + [take(rdi, i, 0) for i in range(3)]
+    dots = functools.reduce(jnp.add, [d * r for d, r in zip(all_dots, scales)]) * share
     for c in range(8):
         sb[pl.ds(c * enc, enc), :] = (pb[c] * (wb[c] - dots)).astype(jnp.bfloat16)
 
@@ -258,13 +259,13 @@
     for e in (2, 3, 1):
         dqb[e] = tn(sb[:, e * block : (e + 1) * block], keys).astype(jnp.bfloat16)
         dq_y[e] = go(remote(dqb.at[e], dqy.at[e], y_send.at[2, e], y_recv.at[2, e], ypeer(NY - e)))
-    mine = tn(sb[:, 0:block], keys)
 
     for c in far_first:
         grad = jnp.dot(sb[pl.ds(c * enc, enc), :], qb[...], preferred_element_type=jnp.float32)
         dkb[c] = grad.astype(jnp.bfloat16)
         back[3].update(give(3, dkb, dko, c))
 
+    mine = tn(sb[:, 0:block], keys)
     for e in range(1, NY):
         dq_y[e].wait_recv()
     mine = (mine + dqy[2].astype(jnp.float32)).astype(jnp.bfloat16)
@@ -299,10 +300,22 @@
         copy.wait()
 
 
-def settle(dq_from, dk_from, dv_from, dq_ref, dk_ref, dv_ref):
-    dq_ref[...] = dq_from[...]
-    dk_ref[...] = dk_from[...]
-    dv_ref[...] = dv_from[...]
+def settle(dq_from, dk_from, dv_from, dq_ref, dk_ref, dv_ref, dqm, dkm, dvm, sem):
+    ins = [
+        pltpu.make_async_copy(src, dst, sem.at[0, i])
+        for i, (src, dst) in enumerate(((dk_from, dkm), (dv_from, dvm), (dq_from, dqm)))
+    ]
+    outs = [
+        pltpu.make_async_copy(src, dst, sem.at[1, i])
+        for i, (src, dst) in enumerate(((dkm, dk_ref), (dvm, dv_ref), (dqm, dq_ref)))
+    ]
+    for copy in ins:
+        copy.start()
+    for copy, out in zip(ins, outs):
+        copy.wait()
+        out.start()
+    for out in outs:
+        out.wait()
 
 
 def body(queries, enc_keys, enc_values, grad_context, enc_lengths):
@@ -352,9 +365,14 @@
             transcendentals=8 * enc * dec,
         ),
     )(enc_lengths, queries[0], enc_keys[0], enc_values[0], grad_context[0])
-    parts = 1
-    specs = tuple(pl.BlockSpec((a.shape[0] // parts, width), lambda i: (i, 0)) for a in outs)
-    dq, dk, dv = pl.pallas_call(settle, grid=(parts,), out_shape=outs, in_specs=specs, out_specs=specs)(*grads)
+    dq, dk, dv = pl.pallas_call(
+        settle,
+        out_shape=outs,
+        in_specs=[any_spec] * 3,
+        out_specs=(any_spec,) * 3,
+        scratch_shapes=[vmem(a.shape, bf16) for a in outs] + [dma((2, 3))],
+        compiler_params=pltpu.CompilerParams(vmem_limit_bytes=56 * 1024 * 1024),
+    )(*grads)
     return (dq[None], dk[None], dv[None])
 
 

time: 71.9 us -> 69.7 us (0.969); the launches traced: 71.7 us -> 68.5 us
  Pallas kernels: 70.4 us -> 67.2 us
    pallas_call x1, Pallas kernels: 68.2 us -> 65.1 us  [body(): pl.pallas_call(kernel, out_shape=outs, in_specs=[pl.BlockSpec(memory_spac...]
where the time goes in v3:
time: 69.7 us; the launch traced here: 68.5 us
  Pallas kernels  67.2 us (96%)
  between operations  1.29 us (2%)
    pallas_call x1, Pallas kernels, body(): pl.pallas_call(kernel, out_shape=outs, in_specs=[pl.BlockSpec(memory_spac...  65.1 us
    pallas_call x1, Pallas kernels, body(): pl.pallas_call(settle, out_shape=outs, in_specs=[any_spec] * 3, out_specs...  2.07 us

profile of v3, /device:TPU:112, one launch (start us, length us, event | category | flops | bytes accessed | tf_op | source)
XLA Modules:
  0.0 68.5 jit_solution(6725097214769234421)
XLA Ops:
  1.3 65.1 %shard_map.76 = (bf16[16,2048]{1,0:T(8,128)(2,1)}, bf16[128,2048]{1,0:T(8,128)(2,1)}, bf16[128,2048]{1,0:T(8,128)(2,1)}) custom-call(s32[1]{0:T(128)S(6)} %copy.8.len_ref, bf16[16,2048]{1,0:T(8,128)(2,1)} %bitcast.11, bf16[128,2048]{1,0:T(8,128)(2,1)} %bitcast.7, bf16[128,2048]{1,0:T(8,128)(2,1)} %bitcast.8, bf16[16,2048]{1,0:T(8,128)(2,1)} %bitcast.12), custom_call_target="tpu_custom_call" | custom-call | flops 1342177280 | bytes 2293760 | tf_op jit(solution)/shard_map/pallas_call | solution.py:337
  66.4 2.1 %shard_map.77 = (bf16[16,2048]{1,0:T(8,128)(2,1)}, bf16[128,2048]{1,0:T(8,128)(2,1)}, bf16[128,2048]{1,0:T(8,128)(2,1)}) custom-call(bf16[16,2048]{1,0:T(8,128)(2,1)} %get-tuple-element.9.dq_from, bf16[128,2048]{1,0:T(8,128)(2,1)} %get-tuple-element.10.dk_from, bf16[128,2048]{1,0:T(8,128)(2,1)} %get-tuple-element.11.dv_from), custom_call_target="tpu_custom_call" | custom-call | tf_op jit(solution)/shard_map/pallas_call | solution.py:368

commit v4 on v3

--- a/solution.py
+++ b/solution.py
@@ -31,7 +31,7 @@
     len_ref, q_hbm, k_hbm, v_hbm, g_hbm,
     dq_ref, dk_ref, dv_ref,
     q_ref, k_ref, v_ref, g_ref, dqo, dko, dvo,
-    qz, gz, qb, gb, kb, vb, pb, wb, sb, dkb, dvb, dqb, dqy, dqz, dqr, mlo, mli, rdo, rdi,
+    qs, q1, gz, qb, gb, kb, vb, pb, wb, sb, dkb, dvb, dqb, dqy, dqz, dqr, mlo, mli, rdo, rdi,
     z_send, z_recv, y_send, y_recv, p_send, p_recv, s_send, s_recv, own,
 ):
     seq = lax.axis_index("seq")
@@ -112,6 +112,14 @@
             for e in (2, 3, 1)
         }
 
+    def q_turn():
+        return {
+            d: go(remote(
+                q1.at[:, (z + d) % GZ], qb.at[:, d], z_send.at[0, d], z_recv.at[0, d], zpeer(d),
+            ))
+            for d in NEAR
+        }
+
     def p_out(kind, src, into):
         out = {}
         for i, (dz, turn) in enumerate(PIECES):
@@ -122,30 +130,35 @@
             ))
         return out
 
-    loads[0].wait()
-    q_in = z_out(0, q_ref, qz)
     loads[1].wait()
     g_in = z_out(1, g_ref, gz)
+    loads[0].wait()
+    for h in range(HEADS):
+        qs[h % 2, h // 2] = q_ref[:, h * dim : (h + 1) * dim]
+    q_in = {
+        e: go(remote(qs.at[(y + e) % 2], q1.at[e], y_send.at[0, e], y_recv.at[0, e], ypeer(e)))
+        for e in (2, 3, 1)
+    }
     loads[2].wait()
-    k_in = p_out(0, k_ref, kb)
     loads[3].wait()
-
-    qz[0:rows, :] = q_ref[:, pair(0)]
+    q1[0] = qs[side]
     gz[0:rows, :] = g_ref[:, pair(0)]
-    for d in reversed(NEAR):
-        q_in[d].wait_recv()
-    q_all = y_out(0, qz, qb)
+    for e in range(1, NY):
+        q_in[e].wait_recv()
+    q_all = q_turn()
     for d in reversed(NEAR):
         g_in[d].wait_recv()
     g_all = y_out(1, gz, gb)
+    k_in = p_out(0, k_ref, kb)
     v_in = p_out(1, v_ref, vb)
 
-    qb[0:block, :] = qz[:, half_of(y)]
+    qb[:, 0] = q1[:, z % GZ]
     gb[0:block, :] = gz[:, half_of(y)]
     kb[0] = k_ref[:, cols(0, y)]
     vb[0] = v_ref[:, cols(0, y)]
-    for e in range(1, NY):
-        q_all[e].wait_recv()
+    for d in reversed(NEAR):
+        q_all[d].wait_recv()
+    queries = qb[...].reshape(dec, dim)
 
     def arrive(copies, c):
         turn, i = divmod(c, 4)
@@ -170,7 +183,7 @@
         live = row + base(first) < length
         if i == 3:
             live = jnp.where(row < half, row + base(-2), row + base(2)) < length
-        scores = jnp.where(live, nt(kb[c], qb[...]), DEAD)
+        scores = jnp.where(live, nt(kb[c], queries), DEAD)
         top = jnp.maximum(jnp.max(scores, axis=0, keepdims=True), FLOOR)
         powers = jnp.exp(scores - top)
         tops[c], sums[c] = top, jnp.sum(powers, axis=0, keepdims=True)
@@ -261,7 +274,7 @@
         dq_y[e] = go(remote(dqb.at[e], dqy.at[e], y_send.at[2, e], y_recv.at[2, e], ypeer(NY - e)))
 
     for c in far_first:
-        grad = jnp.dot(sb[pl.ds(c * enc, enc), :], qb[...], preferred_element_type=jnp.float32)
+        grad = jnp.dot(sb[pl.ds(c * enc, enc), :], qb[...].reshape(dec, dim), preferred_element_type=jnp.float32)
         dkb[c] = grad.astype(jnp.bfloat16)
         back[3].update(give(3, dkb, dko, c))
 
@@ -343,8 +356,8 @@
             vmem((rows, width), bf16), vmem((enc, width), bf16),
             vmem((enc, width), bf16), vmem((rows, width), bf16),
             vmem((rows, width), bf16), vmem((enc, width), bf16), vmem((enc, width), bf16),
-            vmem((block, 2 * dim), bf16), vmem((block, 2 * dim), bf16),
-            vmem((dec, dim), bf16), vmem((dec, dim), bf16),
+            vmem((2, GZ, rows, dim), bf16), vmem((NY, GZ, rows, dim), bf16), vmem((block, 2 * dim), bf16),
+            vmem((NY, NZ, rows, dim), bf16), vmem((dec, dim), bf16),
             vmem((8, enc, dim), bf16), vmem((8, enc, dim), bf16),
             vmem((8, enc, dec), f32), vmem((8, enc, dec), f32),
             vmem((8 * enc, dec), bf16),

time: 69.7 us -> 69.5 us (level)
  no operation moved by 1% of the time
where the time goes in v4:
time: 69.5 us; the launch traced here: 68.2 us
  Pallas kernels  67 us (96%)
  between operations  1.29 us (2%)
    pallas_call x1, Pallas kernels, body(): pl.pallas_call(kernel, out_shape=outs, in_specs=[pl.BlockSpec(memory_spac...  64.9 us
    pallas_call x1, Pallas kernels, body(): pl.pallas_call(settle, out_shape=outs, in_specs=[any_spec] * 3, out_specs...  2.07 us

profile of v4, /device:TPU:112, one launch (start us, length us, event | category | flops | bytes accessed | tf_op | source)
XLA Modules:
  0.0 68.2 jit_solution(1830375683451491413)
XLA Ops:
  1.3 64.9 %shard_map.76 = (bf16[16,2048]{1,0:T(8,128)(2,1)}, bf16[128,2048]{1,0:T(8,128)(2,1)}, bf16[128,2048]{1,0:T(8,128)(2,1)}) custom-call(s32[1]{0:T(128)S(6)} %copy.8.len_ref, bf16[16,2048]{1,0:T(8,128)(2,1)} %bitcast.11, bf16[128,2048]{1,0:T(8,128)(2,1)} %bitcast.7, bf16[128,2048]{1,0:T(8,128)(2,1)} %bitcast.8, bf16[16,2048]{1,0:T(8,128)(2,1)} %bitcast.12), custom_call_target="tpu_custom_call" | custom-call | flops 1342177280 | bytes 2293760 | tf_op jit(solution)/shard_map/pallas_call | solution.py:350
  66.2 2.1 %shard_map.77 = (bf16[16,2048]{1,0:T(8,128)(2,1)}, bf16[128,2048]{1,0:T(8,128)(2,1)}, bf16[128,2048]{1,0:T(8,128)(2,1)}) custom-call(bf16[16,2048]{1,0:T(8,128)(2,1)} %get-tuple-element.9.dq_from, bf16[128,2048]{1,0:T(8,128)(2,1)} %get-tuple-element.10.dk_from, bf16[128,2048]{1,0:T(8,128)(2,1)} %get-tuple-element.11.dv_from), custom_call_target="tpu_custom_call" | custom-call | tf_op jit(solution)/shard_map/pallas_call | solution.py:381
